TPU v7x, 32 devices: a whole 2x2x4 slice. The times are simulated.
32 devices in a mesh: groups: 2 (over y), tok: 4 (over z), col: 4 (over x, core).
Axes of the slice: x: 2, y: 2, z: 4, core: 2. Of those that a mesh axis runs over, the one named last changes fastest.
Arguments:
- attn_out: bfloat16 [512, 8192], P(('groups', 'tok'), 'col'), parts along dimension 0, may hold values from -12 to 12
- residual: bfloat16 [512, 8192], P(('groups', 'col'), 'tok'), parts along dimension 0, may hold values from -310 to 310
- w_out: bfloat16 [8192, 8192], P('col', 'tok'), may hold values from -0.0625 to 0.0625
- norm_gain: float32 [8192], P('tok'), may hold values from 0.5 to 1.5
- rotation: bfloat16 [8192, 8192], P('tok', 'col'), may hold values from -0.23201941 to 0.23201941
Outputs:
- kurtosis: float32 [512], P(('groups', 'tok')), parts along dimension 0
- grad_rot: float32 [16384, 8192], P(('groups', 'tok'), 'col'), parts along dimension 0
There are 2 independent parts, one for each index of `groups`. A program takes and returns all parts, laid end to end along the dimension named above; an argument that names none is the same for every part. Nothing has to cross between parts.
All inputs are finite; a program needn't handle non-finite values.
Results may differ from a plain program's by a relative error of at most 0.0018.
The roundings to bfloat16 on the way count: a program that leaves them out, or rounds other values in their place, can miss the bound.
Values may be sent and summed in bfloat16 or wider, within the bound.
A program may use at most 128 MiB of HBM per device.

v0:
```python
import math

import jax
import jax.numpy as jnp
from jax import lax
from jax.sharding import PartitionSpec as P

norm_eps = 1e-05
moment_eps = 1e-06


def kurtosis_terms(rotated, second, fourth, full_width):
    moment_two = second / full_width + moment_eps
    kurt_vals = fourth / full_width / (moment_two * moment_two)
    cubed = rotated * rotated * rotated
    grad_vals = (
        cubed / (moment_two * moment_two)[:, None] - (kurt_vals / moment_two)[:, None] * rotated
    )
    return (kurt_vals, grad_vals.astype(jnp.bfloat16))


def power_sums(rotated, along):
    squares = rotated * rotated
    return (jnp.sum(squares, axis=along), jnp.sum(squares * squares, axis=along))


def shards(attn_out, residual, w_out, norm_gain, rotation):
    heads_all = lax.all_gather(attn_out, "tok", axis=0, tiled=True)
    row_block = heads_all
    projected = lax.psum_scatter(
        jnp.dot(row_block, w_out, preferred_element_type=jnp.float32),
        "col",
        scatter_dimension=0,
        tiled=True,
    )
    hidden = residual.astype(jnp.float32) + projected
    square_sum = lax.psum(jnp.sum(hidden * hidden, axis=1), "tok")
    full_width = hidden.shape[1] * lax.axis_size("tok")
    row_scale = lax.rsqrt(square_sum / full_width + norm_eps)
    normed = (hidden * row_scale[:, None] * norm_gain[None, :]).astype(jnp.bfloat16)
    normed_all = lax.all_gather(normed, "col", axis=0, tiled=True)
    tokens_total = normed_all.shape[0]
    row_block = normed_all
    rotated = lax.psum_scatter(
        jnp.dot(row_block, rotation, preferred_element_type=jnp.float32),
        "tok",
        scatter_dimension=0,
        tiled=True,
    )
    second, fourth = lax.psum(power_sums(rotated, 1), "col")
    kurt_vals, grad_own = kurtosis_terms(rotated, second, fourth, full_width)
    grad_all = lax.all_gather(grad_own, "tok", axis=0, tiled=True)
    grad_rot = lax.dot_general(
        normed_all, grad_all, (((0,), (0,)), ((), ())), preferred_element_type=jnp.float32
    )
    return (kurt_vals, grad_rot / math.sqrt(tokens_total))


def solution(mesh):
    return jax.shard_map(
        shards,
        mesh=mesh,
        in_specs=(
            P(("groups", "tok"), "col"),
            P(("groups", "col"), "tok"),
            P("col", "tok"),
            P("tok"),
            P("tok", "col"),
        ),
        out_specs=(P(("groups", "tok")), P(("groups", "tok"), "col")),
        check_vma=False,
    )
```

profile of v0, /device:TPU:0, one launch (start us, length us, event | category | flops | bytes accessed | tf_op | source)
XLA Modules:
  0.0 212.4 jit_solution(18247029739795986867)
XLA Ops:
  7.2 0.0 all-gather.4.cloned.1.call-start
  7.2 0.7 all-gather.4.cloned.1.call-update
  7.9 0.0 copy-start.1
  7.9 0.0 copy-start.2
  7.9 0.0 reduce-scatter.3.cloned.1.call-start
  8.0 32.3 %all-gather.4.cloned.1.call-done = bf16[256,2048]{1,0:T(8,128)(2,1)} async-done(((bf16[64,2048]{1,0:T(8,128)(2,1)}), bf16[256,2048]{1,0:T(8,128)(2,1)}) %all-gather.4.cloned.1.call-update) | async-done | bytes 1048592 | tf_op jit(solution)/shard_map/all_gather | solution.py:28
  40.2 7.4 %fusion.5 = f32[256,2048]{1,0:T(8,128)} fusion(bf16[256,2048]{1,0:T(8,128)(2,1)} %all-gather.4.cloned.1.call-done, bf16[2048,2048]{1,0:T(8,128)(2,1)} %param.7), kind=kOutput, calls=%fused_computation.16 | convolution fusion | flops 2147483648 | bytes 11534336 | tf_op jit(solution)/shard_map/dot_general | solution.py:31
  47.6 0.0 reduce-scatter.3.cloned.1.call-update
  47.6 0.0 all-gather.6.cloned.1.call-start
  47.7 31.0 %reduce-scatter.3.cloned.1.call-done = f32[64,2048]{1,0:T(8,128)} async-done(((f32[256,2048]{1,0:T(8,128)}), f32[64,2048]{1,0:T(8,128)}) %reduce-scatter.3.cloned.1.call-update) | async-done | bytes 524304 | tf_op jit(solution)/shard_map/reduce_scatter | solution.py:30
  78.7 0.0 copy-done.1
  78.7 1.2 multiply_reduce_fusion.1
  79.9 11.7 %psum.21 = f32[64]{0:T(128)S(1)} all-reduce(f32[64]{0:T(128)S(1)} %multiply_reduce_fusion.1), channel_id=1, replica_groups=mesh['groups'=2,'tok'=4,'col'=4] {'tok'}, use_global_device_ids=true, to_apply=%region_2.0 | all-reduce | flops 64 | bytes 512 | tf_op jit(solution)/shard_map/psum | solution.py:37
  91.6 0.0 copy-done.2
  91.6 1.9 multiply_convert_fusion
  93.5 0.0 all-gather.6.cloned.1.call-update
  93.5 0.0 reduce-scatter.5.cloned.1.call-start
  93.6 14.1 %all-gather.6.cloned.1.call-done = bf16[256,2048]{1,0:T(8,128)(2,1)} async-done(((bf16[64,2048]{1,0:T(8,128)(2,1)}), bf16[256,2048]{1,0:T(8,128)(2,1)}) %all-gather.6.cloned.1.call-update) | async-done | bytes 1048592 | tf_op jit(solution)/shard_map/all_gather | solution.py:41
  107.6 0.0 copy-start
  107.6 7.4 %fusion.6 = f32[256,2048]{1,0:T(8,128)} fusion(bf16[256,2048]{1,0:T(8,128)(2,1)} %all-gather.6.cloned.1.call-done, bf16[2048,2048]{1,0:T(8,128)(2,1)} %param.9), kind=kOutput, calls=%fused_computation.17 | convolution fusion | flops 2147483648 | bytes 11534336 | tf_op jit(solution)/shard_map/dot_general | solution.py:45
  115.1 0.0 reduce-scatter.5.cloned.1.call-update
  115.1 0.0 all-gather.8.cloned.1.call-start
  115.1 44.0 %reduce-scatter.5.cloned.1.call-done = f32[64,2048]{1,0:T(8,128)} async-done(((f32[256,2048]{1,0:T(8,128)}), f32[64,2048]{1,0:T(8,128)}) %reduce-scatter.5.cloned.1.call-update) | async-done | bytes 524304 | tf_op jit(solution)/shard_map/reduce_scatter | solution.py:44
  159.1 1.2 multiply_reduce_fusion
  160.3 6.4 %all-reduce = (f32[64]{0:T(128)S(1)}, f32[64]{0:T(128)S(1)}) all-reduce(f32[64]{0:T(128)S(1)} %get-tuple-element.3, f32[64]{0:T(128)S(1)} %get-tuple-element.2), channel_id=1, replica_groups=mesh['groups'=2,'tok'=4,'col'=4] {'col'}, use_global_device_ids=true, to_apply=%region_5.0 | all-reduce | flops 128 | bytes 1024 | tf_op jit(solution)/shard_map/psum | solution.py:50
  166.7 0.5 multiply_divide_fusion
  167.2 1.9 fusion.3
  169.1 0.0 all-gather.8.cloned.1.call-update
  169.2 27.0 %all-gather.8.cloned.1.call-done = bf16[256,2048]{1,0:T(8,128)(2,1)} async-done(((bf16[64,2048]{1,0:T(8,128)(2,1)}), bf16[256,2048]{1,0:T(8,128)(2,1)}) %all-gather.8.cloned.1.call-update) | async-done | bytes 1048592 | tf_op jit(solution)/shard_map/all_gather | solution.py:52
  196.1 0.0 copy-done
  196.1 9.8 %convolution_multiply_fusion = f32[2048,2048]{1,0:T(8,128)} fusion(bf16[256,2048]{1,0:T(8,128)(2,1)S(1)} %copy-done, bf16[256,2048]{1,0:T(8,128)(2,1)} %all-gather.8.cloned.1.call-done), kind=kOutput, calls=%fused_computation | convolution fusion | flops 2151677952 | bytes 18874368 | tf_op jit(solution)/shard_map/dot_general | solution.py:53
  (1 shorter events, 0.0 us)
Async XLA Ops:
  7.2 33.1 %all-gather.4.cloned.1.call-start = ((), (), s32[]{:S(2)}) async-start(), calls=%async_computation.2 | async-start | bytes 1310720 | tf_op jit(solution)/shard_map/all_gather | solution.py:28
  7.9 70.8 %copy-start.1 = (bf16[64,2048]{1,0:T(8,128)(2,1)S(1)}, bf16[64,2048]{1,0:T(8,128)(2,1)}, u32[]{:S(2)}) copy-start(bf16[64,2048]{1,0:T(8,128)(2,1)} %param.6) | copy-start | bytes 786436
  7.9 83.7 %copy-start.2 = (f32[2048]{0:T(1024)S(1)}, f32[2048]{0:T(1024)}, u32[]{:S(2)}) copy-start(f32[2048]{0:T(1024)} %param.8) | copy-start | bytes 24580
  7.9 70.8 %reduce-scatter.3.cloned.1.call-start = ((), (), s32[]{:S(2)}) async-start(), calls=%async_computation.3 | async-start | bytes 2621440 | tf_op jit(solution)/shard_map/reduce_scatter | solution.py:30
  47.6 60.0 %all-gather.6.cloned.1.call-start = ((), (), s32[]{:S(2)}) async-start(), calls=%async_computation.4 | async-start | bytes 1310720 | tf_op jit(solution)/shard_map/all_gather | solution.py:41
  93.5 65.6 %reduce-scatter.5.cloned.1.call-start = ((), (), s32[]{:S(2)}) async-start(), calls=%async_computation.5 | async-start | bytes 2621440 | tf_op jit(solution)/shard_map/reduce_scatter | solution.py:44
  107.6 88.5 %copy-start = (bf16[256,2048]{1,0:T(8,128)(2,1)S(1)}, bf16[256,2048]{1,0:T(8,128)(2,1)}, u32[]{:S(2)}) copy-start(bf16[256,2048]{1,0:T(8,128)(2,1)} %all-gather.6.cloned.1.call-done) | copy-start | bytes 3145732
  115.1 81.0 %all-gather.8.cloned.1.call-start = ((), (), s32[]{:S(2)}) async-start(), calls=%async_computation.6 | async-start | bytes 1310720 | tf_op jit(solution)/shard_map/all_gather | solution.py:52
Sparse Core Ops, SparseCore 0:
  9.6 30.6 all-gather.3
  47.7 30.9 reduce-scatter.2
  93.6 13.9 all-gather.5
  115.2 43.8 reduce-scatter.4
  169.3 26.7 all-gather.7
where the time goes:
time: 213 us; the launch traced here: 212 us
  waiting for transfers between devices  149 us (70%)
  matrix products  24.6 us (12%)
  blocking collectives  18.1 us (8%)
  between operations  13.8 us (6%)
  other arithmetic  6.69 us (3%)
    reduce_scatter x1, waiting for transfers between devices, shards(): lax.psum_scatter(jnp.dot(row_block, rotation, preferred_element_type=jnp....  44 us
    all_gather x1, waiting for transfers between devices, shards(): heads_all = lax.all_gather(attn_out, 'tok', axis=0, tiled=True)  32.3 us
    reduce_scatter x1, waiting for transfers between devices, shards(): lax.psum_scatter(jnp.dot(row_block, w_out, preferred_element_type=jnp.flo...  31 us
    all_gather x1, waiting for transfers between devices, shards(): grad_all = lax.all_gather(grad_own, 'tok', axis=0, tiled=True)  27 us
    all_gather x1, waiting for transfers between devices, shards(): normed_all = lax.all_gather(normed, 'col', axis=0, tiled=True)  14.1 us
    psum x1, blocking collectives, shards(): square_sum = lax.psum(jnp.sum(hidden * hidden, axis=1), 'tok')  11.7 us
    dot_general x1, matrix products, shards(): lax.dot_general(normed_all, grad_all, (((0,), (0,)), ((), ())), preferred...  9.77 us
    dot_general x1, matrix products, shards(): jnp.dot(row_block, rotation, preferred_element_type=jnp.float32)  7.44 us
  transfers between devices with their start and end apart: 5, of which 5 were waited for; matrix products, arithmetic and copies ran while one was open for 0% of the time, Pallas kernels for 0%

commit v1 on v0

--- a/solution.py
+++ b/solution.py
@@ -1,8 +1,11 @@
+import functools
 import math
 
 import jax
 import jax.numpy as jnp
 from jax import lax
+from jax.experimental import pallas as pl
+from jax.experimental.pallas import tpu as pltpu
 from jax.sharding import PartitionSpec as P
 
 norm_eps = 1e-05
@@ -56,9 +59,464 @@
     return (kurt_vals, grad_rot / math.sqrt(tokens_total))
 
 
+MESH = pl.DeviceIdType.MESH
+block_order = (0, 2, 1, 3)
+tile_cols = 256
+row_step = 16
+
+
+def rows_loop(count, body):
+    def step(i, carry):
+        body(pl.ds(pl.multiple_of(i * row_step, row_step), row_step))
+        return carry
+
+    lax.fori_loop(0, count // row_step, step, 0)
+
+
+def kernel(
+    full_width,
+    attn_ref, res_ref, gain_ref, w_hbm, rot_hbm,
+    kurt_ref, norm_ref, grad_ref,
+    attn_all, w, rot, part, mate_buf, x_buf, rotp, z_buf, sumsq, stats,
+    load_sem, ag_send, ag_recv, m_send, m_recv, x_send, x_recv, ss_send, ss_recv,
+    n_send, n_recv, z_send, z_recv, st_send, st_recv, g_send, g_recv, k_send, k_recv, k_local,
+):
+    g = lax.axis_index("groups")
+    z = lax.axis_index("tok")
+    c = lax.axis_index("col")
+    core = lax.rem(c, 2)
+    chip = lax.div(c, 2)
+    mate = c + 1 - 2 * core
+    across = lax.rem(c + 2, 4)
+    block, width = attn_ref.shape
+    half = block // 2
+
+    def remote(src, dst, send, recv, to_z, to_c):
+        return pltpu.make_async_remote_copy(
+            src_ref=src, dst_ref=dst, send_sem=send, recv_sem=recv,
+            device_id=(g, to_z, to_c), device_id_type=MESH,
+        )
+
+    load_w = pltpu.make_async_copy(w_hbm, w, load_sem.at[0])
+    load_rot = pltpu.make_async_copy(rot_hbm, rot, load_sem.at[1])
+    load_w.start()
+
+    barrier = pltpu.get_barrier_semaphore()
+    for d in (1, 2, 3):
+        pl.semaphore_signal(barrier, inc=1, device_id=(g, lax.rem(z + d, 4), c), device_id_type=MESH)
+        pl.semaphore_signal(barrier, inc=1, device_id=(g, z, lax.rem(c + d, 4)), device_id_type=MESH)
+    attn_all[z] = attn_ref[...]
+    pl.semaphore_wait(barrier, 6)
+
+    above = jnp.minimum(z + 1, 3)
+    below = jnp.maximum(z - 1, 0)
+    is_end = (z == 0) | (z == 3)
+    is_mid = jnp.logical_not(is_end)
+
+    def ag(s, up):
+        return remote(
+            attn_all.at[s], attn_all.at[s], ag_send.at[up, s], ag_recv.at[s],
+            above if up else below, c,
+        )
+
+    def when(cond):
+        return pl.when(cond)
+
+    @when(z < 3)
+    def _():
+        ag(z, 1).start()
+
+    @when(z > 0)
+    def _():
+        ag(z, 0).start()
+
+    def tiles(left, left_at, right, out):
+        def step(i, carry):
+            cols = pl.ds(pl.multiple_of(i * tile_cols, tile_cols), tile_cols)
+            out[left_at, :, cols] = jnp.dot(
+                left[left_at], right[:, cols], preferred_element_type=jnp.float32
+            )
+            return carry
+
+        lax.fori_loop(0, width // tile_cols, step, 0)
+
+    def mate_copy(s):
+        return remote(
+            part.at[s], mate_buf.at[lax.div(s, 2)], m_send.at[lax.div(s, 2)],
+            m_recv.at[lax.div(s, 2)], z, mate,
+        )
+
+    def x_copy(s):
+        return remote(part.at[s], x_buf, x_send.at[0], x_recv.at[0], z, across)
+
+    def project(s):
+        tiles(attn_all, s, w, part)
+
+        @when(lax.rem(s, 2) != core)
+        def _():
+            mate_copy(s).start()
+
+    def pair_sum(s):
+        @when(lax.rem(s, 2) == core)
+        def _():
+            at = lax.div(s, 2)
+            mate_copy(s).wait_recv()
+
+            def add(rows):
+                part[s, rows, :] += mate_buf[at, rows, :]
+
+            rows_loop(block, add)
+
+            @when(at != chip)
+            def _():
+                x_copy(s).start()
+
+    first = jnp.where(z == 0, 1, z - 1)
+    second = jnp.where(z == 0, 2, jnp.where(z == 3, 1, z + 1))
+    third = jnp.where(z < 2, 3, 0)
+    two_away = jnp.where(z < 2, z + 2, z - 2)
+
+    load_w.wait()
+    load_rot.start()
+    project(z)
+
+    @when(z > 0)
+    def _():
+        ag(below, 1).wait_recv()
+
+        @when(z < 3)
+        def _():
+            ag(below, 1).start()
+
+    @when(z < 3)
+    def _():
+        ag(above, 0).wait_recv()
+
+        @when(z > 0)
+        def _():
+            ag(above, 0).start()
+
+    project(first)
+    pair_sum(z)
+    ag(two_away, 0).wait_recv()
+
+    @when(z == 1)
+    def _():
+        ag(two_away, 0).start()
+
+    @when(z == 2)
+    def _():
+        ag(two_away, 1).start()
+
+    project(second)
+    pair_sum(first)
+
+    @when(is_end)
+    def _():
+        ag(third, 0).wait_recv()
+
+    project(third)
+    pair_sum(second)
+    pair_sum(third)
+
+    x_copy(c).wait_recv()
+
+    def add_residual(rows):
+        hidden = res_ref[rows, :].astype(jnp.float32) + (part[c, rows, :] + x_buf[rows, :])
+        part[c, rows, :] = hidden
+        sumsq[z, rows, :] = jnp.broadcast_to(
+            jnp.sum(hidden * hidden, axis=1, keepdims=True), (row_step, 128)
+        )
+
+    rows_loop(block, add_residual)
+
+    def ss_copy(to_z):
+        return remote(sumsq.at[z], sumsq.at[z], ss_send.at[to_z], ss_recv.at[z], to_z, c)
+
+    def ss_arrival(from_z):
+        return remote(
+            sumsq.at[from_z], sumsq.at[from_z], ss_send.at[from_z], ss_recv.at[from_z], from_z, c
+        )
+
+    for d in (1, 2, 3):
+        ss_copy(lax.rem(z + d, 4)).start()
+    for d in (1, 2, 3):
+        ss_arrival(lax.rem(z + d, 4)).wait_recv()
+
+    def normalise(rows):
+        total = sumsq[0, rows, :] + sumsq[1, rows, :] + sumsq[2, rows, :] + sumsq[3, rows, :]
+        scale = lax.rsqrt(total / full_width + norm_eps)[:, :1]
+        norm_ref[c, rows, :] = (part[c, rows, :] * scale * gain_ref[...]).astype(jnp.bfloat16)
+
+    rows_loop(block, normalise)
+
+    def norm_copy(b, at, to_c):
+        return remote(norm_ref.at[b], norm_ref.at[b], n_send.at[at], n_recv.at[b], z, to_c)
+
+    norm_copy(c, 0, across).start()
+    norm_copy(c, 1, mate).start()
+    load_rot.wait()
+
+    def rotate(b):
+        @when(c != b)
+        def _():
+            norm_copy(b, 0, mate).wait_recv()
+
+        @when(across == b)
+        def _():
+            norm_copy(b, 2, mate).start()
+
+        tiles(norm_ref, b, rot, rotp)
+
+    def z_copy(b, h, to_z):
+        piece = pl.ds(pl.multiple_of(h * half, half), half)
+        return remote(
+            rotp.at[b, piece], z_buf.at[b, h], z_send.at[b, h], z_recv.at[b, h], to_z, c
+        )
+
+    def g_copy(b, h, to_z):
+        piece = pl.ds(pl.multiple_of(h * half, half), half)
+        return remote(
+            grad_ref.at[b, piece], grad_ref.at[b, piece], g_send.at[b, h], g_recv.at[b, h], to_z, c
+        )
+
+    def chain_add(b, h):
+        z_copy(b, h, below).wait_recv()
+
+        def add(i, carry):
+            here = pl.ds(pl.multiple_of(i * row_step, row_step), row_step)
+            there = pl.ds(pl.multiple_of(h * half + i * row_step, row_step), row_step)
+            rotp[b, there, :] += z_buf[b, h, here, :]
+            return carry
+
+        lax.fori_loop(0, half // row_step, add, 0)
+
+    out_half = jnp.where(z == 0, 1, 0)
+    in_half = 1 - out_half
+    inner = jnp.where(z == 0, 1, 2)
+    near = jnp.where(z == 1, 1, 0)
+    far = 1 - near
+    end_z = jnp.where(z == 1, 0, 3)
+    other_mid = jnp.where(z == 1, 2, 1)
+
+    def near_step(b):
+        chain_add(b, near)
+        z_copy(b, near, other_mid).start()
+
+    def far_step(b):
+        chain_add(b, far)
+        z_copy(b, far, end_z).start()
+
+    b0, b1, b2, b3 = block_order
+
+    def stat_copy(b, to_c):
+        return remote(stats.at[b, c], stats.at[b, c], st_send.at[b, to_c], st_recv.at[b, c], z, to_c)
+
+    def stat_arrival(b, from_c):
+        return remote(
+            stats.at[b, from_c], stats.at[b, from_c], st_send.at[b, from_c], st_recv.at[b, from_c],
+            z, from_c,
+        )
+
+    def kurt_copy(b):
+        return remote(
+            stats.at[b, 4, 0], kurt_ref.at[in_half], k_send.at[b], k_recv.at[in_half],
+            jnp.int32(b), c,
+        )
+
+    def finish(b):
+        chain_add(b, in_half)
+
+        def moments(i, carry):
+            here = pl.ds(pl.multiple_of(i * row_step, row_step), row_step)
+            there = pl.ds(pl.multiple_of(in_half * half + i * row_step, row_step), row_step)
+            squares = rotp[b, there, :]
+            squares = squares * squares
+            stats[b, c, 0, here, :] = jnp.broadcast_to(
+                jnp.sum(squares, axis=1, keepdims=True), (row_step, 128)
+            )
+            stats[b, c, 1, here, :] = jnp.broadcast_to(
+                jnp.sum(squares * squares, axis=1, keepdims=True), (row_step, 128)
+            )
+            return carry
+
+        lax.fori_loop(0, half // row_step, moments, 0)
+        for d in (1, 2, 3):
+            stat_copy(b, lax.rem(c + d, 4)).start()
+        for d in (1, 2, 3):
+            stat_arrival(b, lax.rem(c + d, 4)).wait_recv()
+
+        def grads(i, carry):
+            here = pl.ds(pl.multiple_of(i * row_step, row_step), row_step)
+            there = pl.ds(pl.multiple_of(in_half * half + i * row_step, row_step), row_step)
+            sums = [
+                stats[b, 0, q, here, :] + stats[b, 1, q, here, :]
+                + stats[b, 2, q, here, :] + stats[b, 3, q, here, :]
+                for q in (0, 1)
+            ]
+            moment = sums[0] / full_width + moment_eps
+            squared = moment * moment
+            kurt = sums[1] / full_width / squared
+            stats[b, 4, 0, here, :] = kurt
+            cubic = (1.0 / squared)[:, :1]
+            linear = (kurt / moment)[:, :1]
+            rotated = rotp[b, there, :]
+            grad_ref[b, there, :] = (
+                rotated * rotated * rotated * cubic - linear * rotated
+            ).astype(jnp.bfloat16)
+            return carry
+
+        lax.fori_loop(0, half // row_step, grads, 0)
+        g_copy(b, in_half, inner).start()
+
+        @when(z != b)
+        def _():
+            kurt_copy(b).start()
+
+        if b in (0, 3):
+
+            @when(z == b)
+            def _():
+                own = pltpu.make_async_copy(stats.at[b, 4, 0], kurt_ref.at[in_half], k_local.at[0])
+                own.start()
+                own.wait()
+
+    def near_grad(b):
+        g_copy(b, far, other_mid).wait_recv()
+        g_copy(b, far, other_mid).start()
+
+    def far_grad(b):
+        g_copy(b, near, end_z).wait_recv()
+        g_copy(b, near, end_z).start()
+
+    @when(is_end)
+    def _():
+        for b in block_order:
+            rotate(b)
+            z_copy(b, out_half, inner).start()
+        for b in block_order:
+            finish(b)
+        for b in block_order:
+            g_copy(b, out_half, inner).wait_recv()
+
+    @when(is_mid)
+    def _():
+        rotate(b0)
+        rotate(b1)
+        near_step(b0)
+        rotate(b2)
+        near_step(b1)
+        far_step(b0)
+        rotate(b3)
+        near_step(b2)
+        far_step(b1)
+        near_step(b3)
+        far_step(b2)
+        far_step(b3)
+        near_grad(b0)
+        for at in (1, 2, 3):
+            near_grad(block_order[at])
+            far_grad(block_order[at - 1])
+        far_grad(b3)
+
+    def kurt_arrival(h):
+        return remote(
+            stats.at[0, 4, 0], kurt_ref.at[h], k_send.at[0], k_recv.at[h], jnp.int32(3 * h), c
+        )
+
+    @when(z != 0)
+    def _():
+        kurt_arrival(0).wait_recv()
+
+    @when(z != 3)
+    def _():
+        kurt_arrival(1).wait_recv()
+
+    for s in range(4):
+
+        @when((s <= z) & (z < 3))
+        def _():
+            ag(s, 1).wait_send()
+
+        @when((s >= z) & (z > 0))
+        def _():
+            ag(s, 0).wait_send()
+
+        @when(core != s % 2)
+        def _():
+            mate_copy(jnp.int32(s)).wait_send()
+
+        @when(is_mid)
+        def _():
+            for h in (0, 1):
+                z_copy(s, h, below).wait_send()
+                g_copy(s, h, below).wait_send()
+
+        @when(is_end)
+        def _():
+            z_copy(s, out_half, inner).wait_send()
+            g_copy(s, in_half, inner).wait_send()
+            for d in (1, 2, 3):
+                stat_copy(s, lax.rem(c + d, 4)).wait_send()
+
+            @when(z != s)
+            def _():
+                kurt_copy(s).wait_send()
+
+    x_copy(across).wait_send()
+    for d in (1, 2, 3):
+        ss_copy(lax.rem(z + d, 4)).wait_send()
+    norm_copy(c, 0, across).wait_send()
+    norm_copy(c, 1, mate).wait_send()
+    norm_copy(across, 2, mate).wait_send()
+
+
+def fused_shards(attn_out, residual, w_out, norm_gain, rotation):
+    block, width = attn_out.shape
+    full_width = width * 4
+    half = block // 2
+    dma = pltpu.SemaphoreType.DMA
+    vmem = pl.BlockSpec(memory_space=pltpu.VMEM)
+    kurt, normed, grads = pl.pallas_call(
+        functools.partial(kernel, full_width),
+        out_shape=(
+            jax.ShapeDtypeStruct((2, half, 128), jnp.float32),
+            jax.ShapeDtypeStruct((4, block, width), jnp.bfloat16),
+            jax.ShapeDtypeStruct((4, block, width), jnp.bfloat16),
+        ),
+        in_specs=[vmem, vmem, vmem, pl.BlockSpec(memory_space=pl.ANY), pl.BlockSpec(memory_space=pl.ANY)],
+        out_specs=(vmem, vmem, vmem),
+        scratch_shapes=[
+            pltpu.VMEM((4, block, width), jnp.bfloat16),
+            pltpu.VMEM(w_out.shape, jnp.bfloat16),
+            pltpu.VMEM(rotation.shape, jnp.bfloat16),
+            pltpu.VMEM((4, block, width), jnp.float32),
+            pltpu.VMEM((2, block, width), jnp.float32),
+            pltpu.VMEM((block, width), jnp.float32),
+            pltpu.VMEM((4, block, width), jnp.float32),
+            pltpu.VMEM((4, 2, half, width), jnp.float32),
+            pltpu.VMEM((4, block, 128), jnp.float32),
+            pltpu.VMEM((4, 5, 2, half, 128), jnp.float32),
+            dma((2,)), dma((2, 4)), dma((4,)), dma((2,)), dma((2,)), dma((1,)), dma((1,)),
+            dma((4,)), dma((4,)), dma((3,)), dma((4,)), dma((4, 2)), dma((4, 2)),
+            dma((4, 4)), dma((4, 4)), dma((4, 2)), dma((4, 2)), dma((4,)), dma((2,)), dma((1,)),
+        ],
+        compiler_params=pltpu.CompilerParams(
+            collective_id=0, has_side_effects=True, vmem_limit_bytes=48 * 1024 * 1024
+        ),
+    )(attn_out, residual, norm_gain.reshape(1, width), w_out, rotation)
+    normed = normed.reshape(4 * block, width)
+    grads = grads.reshape(4 * block, width)
+    grad_rot = lax.dot_general(
+        normed, grads, (((0,), (0,)), ((), ())), preferred_element_type=jnp.float32
+    )
+    return (kurt[:, :, 0].reshape(block), grad_rot / math.sqrt(4 * block))
+
+
 def solution(mesh):
+    fits = mesh.shape["tok"] == 4 and mesh.shape["col"] == 4
     return jax.shard_map(
-        shards,
+        fused_shards if fits else shards,
         mesh=mesh,
         in_specs=(
             P(("groups", "tok"), "col"),

time: 213 us -> 121 us (0.57)
  waiting for transfers between devices: 149 us -> 0 us
  Pallas kernels: 0 us -> 109 us
  blocking collectives: 18.1 us -> 0 us
  matrix products: 24.6 us -> 8.54 us
  between operations: 13.8 us -> 0.65 us
  other arithmetic: 6.69 us -> 0 us
  local copies, waits for them, and re-layouts: 0.01 us -> 3.28 us
    pallas_call x0 -> x1, Pallas kernels: none -> 109 us  [fused_shards(): pl.pallas_call(functools.partial(kernel, full_width), out_shape=(jax.Shap...]
    reduce_scatter x2 -> x0, waiting for transfers between devices: 75 us -> none  [the longest x1 44 us: shards(): lax.psum_scatter(jnp.dot(row_block, rotation, preferred_element_type=jnp....]
    all_gather x3 -> x0, waiting for transfers between devices: 73.3 us -> none  [the longest x1 32.3 us: shards(): heads_all = lax.all_gather(attn_out, 'tok', axis=0, tiled=True)]
    psum x2 -> x0, blocking collectives: 18.1 us -> none  [the longest x1 11.7 us: shards(): square_sum = lax.psum(jnp.sum(hidden * hidden, axis=1), 'tok')]
    dot_general x3 -> x1, matrix products: 24.6 us -> 8.54 us  [fused_shards(): lax.dot_general(normed, grads, (((0,), (0,)), ((), ())), preferred_elemen...]
    convert_element_type x2 -> x0, other arithmetic: 3.74 us -> none  [the longest x1 1.88 us: kurtosis_terms(): return (kurt_vals, grad_vals.astype(jnp.bfloat16))]
    unnamed x6, local copies, waits for them, and re-layouts: 0.01 us -> 2.59 us
    reduce_sum x2 -> x0, other arithmetic: 2.42 us -> none  [the longest x1 1.21 us: shards(): square_sum = lax.psum(jnp.sum(hidden * hidden, axis=1), 'tok')]
  transfers between devices with their start and end apart: 5 -> 0, of which waited for: 5 -> 0; matrix products, arithmetic and copies ran while one was open for 0% -> 0% of each run, Pallas kernels for 0% -> 0%
where the time goes in v1:
time: 121 us
  Pallas kernels  109 us (90%)
  matrix products  8.54 us (7%)
  local copies, waits for them, and re-layouts  3.28 us (3%)
    pallas_call x1, Pallas kernels, fused_shards(): pl.pallas_call(functools.partial(kernel, full_width), out_shape=(jax.Shap...  109 us
    dot_general x1, matrix products, fused_shards(): lax.dot_general(normed, grads, (((0,), (0,)), ((), ())), preferred_elemen...  8.54 us
    unnamed x6, local copies, waits for them, and re-layouts  2.59 us

profile of v1, /device:TPU:0, one launch (start us, length us, event | category | flops | bytes accessed | tf_op | source)
XLA Modules:
  0.0 121.2 jit_solution(15914384045385990912)
XLA Ops:
  0.6 0.0 copy-start
  0.6 0.9 copy-done
  1.6 0.0 copy-start.1
  1.6 0.9 copy-done.1
  2.5 0.0 copy-start.2
  2.5 0.7 copy-done.2
  3.2 108.7 %shard_map.68 = (f32[2,32,128]{2,1,0:T(8,128)S(1)}, bf16[4,64,2048]{2,1,0:T(8,128)(2,1)S(1)}, bf16[4,64,2048]{2,1,0:T(8,128)(2,1)S(1)}) custom-call(bf16[64,2048]{1,0:T(8,128)(2,1)S(1)} %copy-done, bf16[64,2048]{1,0:T(8,128)(2,1)S(1)} %copy-done.1, f32[1,2048]{1,0:T(1,128)S(1)} %bitcast.5, bf16[2048,2048]{1,0:T(8,128)(2,1)} %w_hbm.1, bf16[2048,2048]{1,0:T(8,128)(2,1)} %rot_hbm.1), custom_call_target="tpu_custom_call" | custom-call | tf_op jit(solution)/shard_map/pallas_call | solution.py:480
  112.0 0.1 slice_reduce_fusion
  112.0 0.6 reshape_squeeze.3
  112.6 8.5 %bitcast_multiply_fusion = f32[2048,2048]{1,0:T(8,128)} fusion(bf16[4,64,2048]{2,1,0:T(8,128)(2,1)S(1)} %get-tuple-element.6, bf16[4,64,2048]{2,1,0:T(8,128)(2,1)S(1)} %get-tuple-element.7), kind=kOutput, calls=%fused_computation | convolution fusion | flops 2151677952 | bytes 18874368 | tf_op jit(solution)/shard_map/dot_general | solution.py:510
Async XLA Ops:
  0.6 1.0 copy-start
  1.6 0.9 copy-start.1
  2.5 0.7 copy-start.2

commit v2 on v1

v2 whole, which is shorter than its diff:
```python
import functools
import math

import jax
import jax.numpy as jnp
from jax import lax
from jax.experimental import pallas as pl
from jax.experimental.pallas import tpu as pltpu
from jax.sharding import PartitionSpec as P

norm_eps = 1e-05
moment_eps = 1e-06


def kurtosis_terms(rotated, second, fourth, full_width):
    moment_two = second / full_width + moment_eps
    kurt_vals = fourth / full_width / (moment_two * moment_two)
    cubed = rotated * rotated * rotated
    grad_vals = (
        cubed / (moment_two * moment_two)[:, None] - (kurt_vals / moment_two)[:, None] * rotated
    )
    return (kurt_vals, grad_vals.astype(jnp.bfloat16))


def power_sums(rotated, along):
    squares = rotated * rotated
    return (jnp.sum(squares, axis=along), jnp.sum(squares * squares, axis=along))


def shards(attn_out, residual, w_out, norm_gain, rotation):
    heads_all = lax.all_gather(attn_out, "tok", axis=0, tiled=True)
    row_block = heads_all
    projected = lax.psum_scatter(
        jnp.dot(row_block, w_out, preferred_element_type=jnp.float32),
        "col",
        scatter_dimension=0,
        tiled=True,
    )
    hidden = residual.astype(jnp.float32) + projected
    square_sum = lax.psum(jnp.sum(hidden * hidden, axis=1), "tok")
    full_width = hidden.shape[1] * lax.axis_size("tok")
    row_scale = lax.rsqrt(square_sum / full_width + norm_eps)
    normed = (hidden * row_scale[:, None] * norm_gain[None, :]).astype(jnp.bfloat16)
    normed_all = lax.all_gather(normed, "col", axis=0, tiled=True)
    tokens_total = normed_all.shape[0]
    row_block = normed_all
    rotated = lax.psum_scatter(
        jnp.dot(row_block, rotation, preferred_element_type=jnp.float32),
        "tok",
        scatter_dimension=0,
        tiled=True,
    )
    second, fourth = lax.psum(power_sums(rotated, 1), "col")
    kurt_vals, grad_own = kurtosis_terms(rotated, second, fourth, full_width)
    grad_all = lax.all_gather(grad_own, "tok", axis=0, tiled=True)
    grad_rot = lax.dot_general(
        normed_all, grad_all, (((0,), (0,)), ((), ())), preferred_element_type=jnp.float32
    )
    return (kurt_vals, grad_rot / math.sqrt(tokens_total))


MESH = pl.DeviceIdType.MESH
block_order = (0, 2, 1, 3)
tile_cols = 256
row_step = 16


def rows_loop(count, body):
    def step(i, carry):
        body(pl.ds(pl.multiple_of(i * row_step, row_step), row_step))
        return carry

    lax.fori_loop(0, count // row_step, step, 0)


def kernel(
    full_width,
    attn_hbm, res_hbm, gain_hbm, w_hbm, rot_hbm,
    kurt_ref, norm_ref, grad_ref,
    res_ref, gain_ref, attn_all, w, rot, part, mate_buf, x_buf, rotp, z_buf, sumsq, stats,
    load_sem, ag_send, ag_recv, m_send, m_recv, x_send, x_recv, ss_send, ss_recv,
    n_send, n_recv, z_send, z_recv, st_send, st_recv, g_send, g_recv, k_send, k_recv,
):
    g = lax.axis_index("groups")
    z = lax.axis_index("tok")
    c = lax.axis_index("col")
    core = lax.rem(c, 2)
    chip = lax.div(c, 2)
    mate = c + 1 - 2 * core
    across = lax.rem(c + 2, 4)
    block, width = attn_hbm.shape
    half = block // 2
    quarter = half // 2
    half_cols = width // 2

    def remote(src, dst, send, recv, to_z, to_c):
        return pltpu.make_async_remote_copy(
            src_ref=src, dst_ref=dst, send_sem=send, recv_sem=recv,
            device_id=(g, to_z, to_c), device_id_type=MESH,
        )

    def side(q):
        return pl.ds(q * half_cols, half_cols)

    load_attn = pltpu.make_async_copy(attn_hbm, attn_all.at[z], load_sem.at[0])
    load_w = [
        pltpu.make_async_copy(w_hbm.at[:, side(q)], w.at[:, side(q)], load_sem.at[1 + q])
        for q in (0, 1)
    ]
    load_rot = pltpu.make_async_copy(rot_hbm, rot, load_sem.at[3])
    load_res = pltpu.make_async_copy(res_hbm, res_ref, load_sem.at[4])
    load_gain = pltpu.make_async_copy(gain_hbm, gain_ref, load_sem.at[5])
    load_attn.start()
    load_w[0].start()
    load_w[1].start()

    barrier = pltpu.get_barrier_semaphore()
    for d in (1, 2, 3):
        pl.semaphore_signal(barrier, inc=1, device_id=(g, lax.rem(z + d, 4), c), device_id_type=MESH)
        pl.semaphore_signal(barrier, inc=1, device_id=(g, z, lax.rem(c + d, 4)), device_id_type=MESH)
    pl.semaphore_wait(barrier, 6)

    above = jnp.minimum(z + 1, 3)
    below = jnp.maximum(z - 1, 0)
    is_end = (z == 0) | (z == 3)
    is_mid = jnp.logical_not(is_end)

    def ag(s, up):
        return remote(
            attn_all.at[s], attn_all.at[s], ag_send.at[up, s], ag_recv.at[s],
            above if up else below, c,
        )

    def when(cond):
        return pl.when(cond)

    def ag_own(up):
        return remote(
            attn_hbm, attn_all.at[z], ag_send.at[up, z], ag_recv.at[z],
            above if up else below, c,
        )

    @when(z < 3)
    def _():
        ag_own(1).start()

    @when(z > 0)
    def _():
        ag_own(0).start()

    def tiles(left, left_at, right, out, q):
        def step(i, carry):
            cols = pl.ds(pl.multiple_of(q * half_cols + i * tile_cols, tile_cols), tile_cols)
            out[left_at, :, cols] = jnp.dot(
                left[left_at], right[:, cols], preferred_element_type=jnp.float32
            )
            return carry

        lax.fori_loop(0, half_cols // tile_cols, step, 0)

    def mate_copy(s, q):
        at = lax.div(s, 2)
        return remote(
            part.at[s, :, side(q)], mate_buf.at[at, :, side(q)], m_send.at[at, q],
            m_recv.at[at, q], z, mate,
        )

    def x_copy(s, q):
        return remote(
            part.at[s, :, side(q)], x_buf.at[:, side(q)], x_send.at[q], x_recv.at[q], z, across
        )

    def project(s, q):
        tiles(attn_all, s, w, part, q)

        @when(lax.rem(s, 2) != core)
        def _():
            mate_copy(s, q).start()

    def pair_sum(s, q):
        @when(lax.rem(s, 2) == core)
        def _():
            at = lax.div(s, 2)
            mate_copy(s, q).wait_recv()

            def add(rows):
                part[s, rows, side(q)] += mate_buf[at, rows, side(q)]

            rows_loop(block, add)

            @when(at != chip)
            def _():
                x_copy(s, q).start()

    first = jnp.where(z == 0, 1, z - 1)
    second = jnp.where(z == 0, 2, jnp.where(z == 3, 1, z + 1))
    third = jnp.where(z < 2, 3, 0)
    two_away = jnp.where(z < 2, z + 2, z - 2)

    load_attn.wait()
    load_w[0].wait()
    load_rot.start()
    load_res.start()
    load_gain.start()
    project(z, 0)

    @when(z > 0)
    def _():
        ag(below, 1).wait_recv()

        @when(z < 3)
        def _():
            ag(below, 1).start()

    @when(z < 3)
    def _():
        ag(above, 0).wait_recv()

        @when(z > 0)
        def _():
            ag(above, 0).start()

    load_w[1].wait()
    project(z, 1)
    pair_sum(z, 0)
    project(first, 0)
    pair_sum(z, 1)
    project(first, 1)
    pair_sum(first, 0)
    ag(two_away, 0).wait_recv()

    @when(z == 1)
    def _():
        ag(two_away, 0).start()

    @when(z == 2)
    def _():
        ag(two_away, 1).start()

    project(second, 0)
    pair_sum(first, 1)
    project(second, 1)
    pair_sum(second, 0)

    @when(is_end)
    def _():
        pair_sum(second, 1)
        ag(third, 0).wait_recv()

    project(third, 0)

    @when(is_mid)
    def _():
        pair_sum(second, 1)

    project(third, 1)
    pair_sum(third, 0)
    pair_sum(third, 1)

    load_res.wait()
    load_gain.wait()
    x_copy(c, 0).wait_recv()
    x_copy(c, 1).wait_recv()

    def add_residual(rows):
        hidden = res_ref[rows, :].astype(jnp.float32) + (part[c, rows, :] + x_buf[rows, :])
        part[c, rows, :] = hidden
        sumsq[z, rows, :] = jnp.broadcast_to(
            jnp.sum(hidden * hidden, axis=1, keepdims=True), (row_step, 128)
        )

    rows_loop(block, add_residual)

    def ss_copy(to_z):
        return remote(sumsq.at[z], sumsq.at[z], ss_send.at[to_z], ss_recv.at[z], to_z, c)

    def ss_arrival(from_z):
        return remote(
            sumsq.at[from_z], sumsq.at[from_z], ss_send.at[from_z], ss_recv.at[from_z], from_z, c
        )

    for d in (1, 2, 3):
        ss_copy(lax.rem(z + d, 4)).start()
    for d in (1, 2, 3):
        ss_arrival(lax.rem(z + d, 4)).wait_recv()

    def normalise(rows):
        total = sumsq[0, rows, :] + sumsq[1, rows, :] + sumsq[2, rows, :] + sumsq[3, rows, :]
        scale = lax.rsqrt(total / full_width + norm_eps)[:, :1]
        norm_ref[c, rows, :] = (part[c, rows, :] * scale * gain_ref[...]).astype(jnp.bfloat16)

    rows_loop(block, normalise)

    def norm_copy(b, at, to_c):
        return remote(norm_ref.at[b], norm_ref.at[b], n_send.at[at], n_recv.at[b], z, to_c)

    norm_copy(c, 0, across).start()
    norm_copy(c, 1, mate).start()
    load_rot.wait()

    def rotate(b, q):
        if q == 0:

            @when(c != b)
            def _():
                norm_copy(b, 0, mate).wait_recv()

            @when(across == b)
            def _():
                norm_copy(b, 2, mate).start()

        tiles(norm_ref, b, rot, rotp, q)

    def piece(h, q):
        return pl.ds(pl.multiple_of(h * half + q * quarter, quarter), quarter)

    def z_copy(u, h, to_z):
        b, q = u
        return remote(
            rotp.at[b, piece(h, q)], z_buf.at[b, h, q], z_send.at[b, h, q], z_recv.at[b, h, q],
            to_z, c,
        )

    def g_copy(u, h, to_z):
        b, q = u
        return remote(
            grad_ref.at[b, piece(h, q)], grad_ref.at[b, piece(h, q)], g_send.at[b, h, q],
            g_recv.at[b, h, q], to_z, c,
        )

    def chain_add(u, h):
        b, q = u
        z_copy(u, h, below).wait_recv()
        rotp[b, piece(h, q), :] += z_buf[b, h, q]

    out_half = jnp.where(z == 0, 1, 0)
    in_half = 1 - out_half
    inner = jnp.where(z == 0, 1, 2)
    near = jnp.where(z == 1, 1, 0)
    far = 1 - near
    end_z = jnp.where(z == 1, 0, 3)
    other_mid = jnp.where(z == 1, 2, 1)
    units = [(b, q) for b in block_order for q in (0, 1)]
    last = len(units)

    def near_step(i):
        if 0 <= i < last:
            chain_add(units[i], near)
            z_copy(units[i], near, other_mid).start()

    def far_step(i):
        if 0 <= i < last:
            chain_add(units[i], far)
            z_copy(units[i], far, end_z).start()

    def stat_copy(u, to_c):
        b, q = u
        return remote(
            stats.at[b, q, c], stats.at[b, q, c], st_send.at[b, q, to_c], st_recv.at[b, q, c],
            z, to_c,
        )

    def stat_arrival(u, from_c):
        b, q = u
        return remote(
            stats.at[b, q, from_c], stats.at[b, q, from_c], st_send.at[b, q, from_c],
            st_recv.at[b, q, from_c], z, from_c,
        )

    def kurt_copy(u):
        b, q = u
        return remote(
            stats.at[b, q, 4, 0], kurt_ref.at[in_half, q], k_send.at[b, q], k_recv.at[in_half, q],
            jnp.int32(b), c,
        )

    def moments(u):
        b, q = u
        chain_add(u, in_half)
        squares = rotp[b, piece(in_half, q), :]
        squares = squares * squares
        stats[b, q, c, 0] = jnp.broadcast_to(
            jnp.sum(squares, axis=1, keepdims=True), (quarter, 128)
        )
        stats[b, q, c, 1] = jnp.broadcast_to(
            jnp.sum(squares * squares, axis=1, keepdims=True), (quarter, 128)
        )
        for d in (1, 2, 3):
            stat_copy(u, lax.rem(c + d, 4)).start()

    def finish(u):
        b, q = u
        for d in (1, 2, 3):
            stat_arrival(u, lax.rem(c + d, 4)).wait_recv()
        sums = [
            stats[b, q, 0, p] + stats[b, q, 1, p] + stats[b, q, 2, p] + stats[b, q, 3, p]
            for p in (0, 1)
        ]
        moment = sums[0] / full_width + moment_eps
        squared = moment * moment
        kurt = sums[1] / full_width / squared
        stats[b, q, 4, 0] = kurt
        cubic = (1.0 / squared)[:, :1]
        linear = (kurt / moment)[:, :1]
        rotated = rotp[b, piece(in_half, q), :]
        grad_ref[b, piece(in_half, q), :] = (
            rotated * rotated * rotated * cubic - linear * rotated
        ).astype(jnp.bfloat16)
        g_copy(u, in_half, inner).start()

        @when(z != b)
        def _():
            kurt_copy(u).start()

        if b in (0, 3):

            @when(z == b)
            def _():
                kurt_ref[in_half, q] = kurt

    def near_grad(i):
        if 0 <= i < last:
            g_copy(units[i], far, other_mid).wait_recv()
            g_copy(units[i], far, other_mid).start()

    def far_grad(i):
        if 0 <= i < last:
            g_copy(units[i], near, end_z).wait_recv()
            g_copy(units[i], near, end_z).start()

    @when(is_end)
    def _():
        for b in block_order:
            rotate(b, 0)
            rotate(b, 1)
            for q in (0, 1):
                z_copy((b, q), out_half, inner).start()
        for i, u in enumerate(units):
            moments(u)
            if i > 0:
                finish(units[i - 1])
        finish(units[-1])
        for u in units:
            g_copy(u, out_half, inner).wait_recv()

    @when(is_mid)
    def _():
        for b in block_order[:2]:
            rotate(b, 0)
            rotate(b, 1)
        later = [(b, q) for b in block_order[2:] for q in (0, 1)]
        for i in range(last + 8):
            near_step(i)
            far_step(i - 1)
            near_grad(i - 6)
            far_grad(i - 7)
            if i < len(later):
                rotate(*later[i])

    def kurt_arrival(h, q):
        return remote(
            stats.at[0, q, 4, 0], kurt_ref.at[h, q], k_send.at[0, q], k_recv.at[h, q],
            jnp.int32(3 * h), c,
        )

    for q in (0, 1):

        @when(z != 0)
        def _():
            kurt_arrival(0, q).wait_recv()

        @when(z != 3)
        def _():
            kurt_arrival(1, q).wait_recv()

    for s in range(4):

        @when((s <= z) & (z < 3))
        def _():
            ag(s, 1).wait_send()

        @when((s >= z) & (z > 0))
        def _():
            ag(s, 0).wait_send()

        for q in (0, 1):

            @when(core != s % 2)
            def _():
                mate_copy(jnp.int32(s), q).wait_send()

            u = (s, q)

            @when(is_mid)
            def _():
                for h in (0, 1):
                    z_copy(u, h, below).wait_send()
                    g_copy(u, h, below).wait_send()

            @when(is_end)
            def _():
                z_copy(u, out_half, inner).wait_send()
                g_copy(u, in_half, inner).wait_send()
                for d in (1, 2, 3):
                    stat_copy(u, lax.rem(c + d, 4)).wait_send()

                @when(z != s)
                def _():
                    kurt_copy(u).wait_send()

    for q in (0, 1):
        x_copy(across, q).wait_send()
    for d in (1, 2, 3):
        ss_copy(lax.rem(z + d, 4)).wait_send()
    norm_copy(c, 0, across).wait_send()
    norm_copy(c, 1, mate).wait_send()
    norm_copy(across, 2, mate).wait_send()


def fused_shards(attn_out, residual, w_out, norm_gain, rotation):
    block, width = attn_out.shape
    full_width = width * 4
    quarter = block // 4
    dma = pltpu.SemaphoreType.DMA
    vmem = pl.BlockSpec(memory_space=pltpu.VMEM)
    kurt, normed, grads = pl.pallas_call(
        functools.partial(kernel, full_width),
        out_shape=(
            jax.ShapeDtypeStruct((2, 2, quarter, 128), jnp.float32),
            jax.ShapeDtypeStruct((4, block, width), jnp.bfloat16),
            jax.ShapeDtypeStruct((4, block, width), jnp.bfloat16),
        ),
        in_specs=[pl.BlockSpec(memory_space=pltpu.HBM)] * 5,
        out_specs=(vmem, vmem, vmem),
        scratch_shapes=[
            pltpu.VMEM((block, width), jnp.bfloat16),
            pltpu.VMEM((1, width), jnp.float32),
            pltpu.VMEM((4, block, width), jnp.bfloat16),
            pltpu.VMEM(w_out.shape, jnp.bfloat16),
            pltpu.VMEM(rotation.shape, jnp.bfloat16),
            pltpu.VMEM((4, block, width), jnp.float32),
            pltpu.VMEM((2, block, width), jnp.float32),
            pltpu.VMEM((block, width), jnp.float32),
            pltpu.VMEM((4, block, width), jnp.float32),
            pltpu.VMEM((4, 2, 2, quarter, width), jnp.float32),
            pltpu.VMEM((4, block, 128), jnp.float32),
            pltpu.VMEM((4, 2, 5, 2, quarter, 128), jnp.float32),
            dma((6,)), dma((2, 4)), dma((4,)), dma((2, 2)), dma((2, 2)), dma((2,)), dma((2,)),
            dma((4,)), dma((4,)), dma((3,)), dma((4,)), dma((4, 2, 2)), dma((4, 2, 2)),
            dma((4, 2, 4)), dma((4, 2, 4)), dma((4, 2, 2)), dma((4, 2, 2)), dma((4, 2)), dma((2, 2)),
        ],
        compiler_params=pltpu.CompilerParams(
            collective_id=0, has_side_effects=True, vmem_limit_bytes=60 * 1024 * 1024
        ),
    )(attn_out, residual, norm_gain.reshape(1, width), w_out, rotation)
    normed = normed.reshape(4 * block, width)
    grads = grads.reshape(4 * block, width)
    grad_rot = lax.dot_general(
        normed, grads, (((0,), (0,)), ((), ())), preferred_element_type=jnp.float32
    )
    return (kurt[:, :, :, 0].reshape(block), grad_rot / math.sqrt(4 * block))


def solution(mesh):
    fits = mesh.shape["tok"] == 4 and mesh.shape["col"] == 4
    return jax.shard_map(
        fused_shards if fits else shards,
        mesh=mesh,
        in_specs=(
            P(("groups", "tok"), "col"),
            P(("groups", "col"), "tok"),
            P("col", "tok"),
            P("tok"),
            P("tok", "col"),
        ),
        out_specs=(P(("groups", "tok")), P(("groups", "tok"), "col")),
        check_vma=False,
    )
```

time: 121 us -> 115 us (0.950)
  Pallas kernels: 109 us -> 103 us
  local copies, waits for them, and re-layouts: 3.28 us -> 1.45 us
  matrix products: 8.54 us -> 10.1 us
    pallas_call x1, Pallas kernels: 109 us -> 103 us  [fused_shards(): pl.pallas_call(functools.partial(kernel, full_width), out_shape=(jax.Shap...]
    unnamed x6 -> x0, local copies, waits for them, and re-layouts: 2.59 us -> none
    dot_general x1, matrix products: 8.54 us -> 10.1 us  [fused_shards(): lax.dot_general(normed, grads, (((0,), (0,)), ((), ())), preferred_elemen...]
where the time goes in v2:
time: 115 us
  Pallas kernels  103 us (90%)
  matrix products  10.1 us (9%)
  local copies, waits for them, and re-layouts  1.45 us (1%)
    pallas_call x1, Pallas kernels, fused_shards(): pl.pallas_call(functools.partial(kernel, full_width), out_shape=(jax.Shap...  103 us
    dot_general x1, matrix products, fused_shards(): lax.dot_general(normed, grads, (((0,), (0,)), ((), ())), preferred_elemen...  10.1 us

profile of v2, /device:TPU:0, one launch (start us, length us, event | category | flops | bytes accessed | tf_op | source)
XLA Modules:
  0.0 115.1 jit_solution(16857172303622325831)
XLA Ops:
  0.6 102.9 %shard_map.68 = (f32[2,2,16,128]{3,2,1,0:T(8,128)}, bf16[4,64,2048]{2,1,0:T(8,128)(2,1)}, bf16[4,64,2048]{2,1,0:T(8,128)(2,1)}) custom-call(bf16[64,2048]{1,0:T(8,128)(2,1)} %attn_hbm.1, bf16[64,2048]{1,0:T(8,128)(2,1)} %res_hbm.1, f32[1,2048]{1,0:T(1,128)} %bitcast.5, bf16[2048,2048]{1,0:T(8,128)(2,1)} %w_hbm.1, bf16[2048,2048]{1,0:T(8,128)(2,1)} %rot_hbm.1), custom_call_target="tpu_custom_call" | custom-call | tf_op jit(solution)/shard_map/pallas_call | solution.py:526
  103.5 0.8 slice_reduce_fusion
  104.4 0.6 reshape_squeeze.3
  105.0 10.1 %bitcast_multiply_fusion = f32[2048,2048]{1,0:T(8,128)} fusion(bf16[4,64,2048]{2,1,0:T(8,128)(2,1)} %get-tuple-element.6, bf16[4,64,2048]{2,1,0:T(8,128)(2,1)} %get-tuple-element.7), kind=kOutput, calls=%fused_computation | convolution fusion | flops 2151677952 | bytes 18874368 | tf_op jit(solution)/shard_map/dot_general | solution.py:558

commit v3 on v2

--- a/solution.py
+++ b/solution.py
@@ -63,6 +63,8 @@
 block_order = (0, 2, 1, 3)
 tile_cols = 256
 row_step = 16
+outer_rows = 256
+outer_cols = 512
 
 
 def rows_loop(count, body):
@@ -79,7 +81,7 @@
     kurt_ref, norm_ref, grad_ref,
     res_ref, gain_ref, attn_all, w, rot, part, mate_buf, x_buf, rotp, z_buf, sumsq, stats,
     load_sem, ag_send, ag_recv, m_send, m_recv, x_send, x_recv, ss_send, ss_recv,
-    n_send, n_recv, z_send, z_recv, st_send, st_recv, g_send, g_recv, k_send, k_recv,
+    n_send, n_recv, z_send, z_recv, st_send, st_recv, g_send, g_recv, k_send, k_recv, direct_send,
 ):
     g = lax.axis_index("groups")
     z = lax.axis_index("tok")
@@ -140,6 +142,11 @@
             above if up else below, c,
         )
 
+    def ag_direct():
+        return remote(
+            attn_all.at[z], attn_all.at[z], direct_send.at[0], ag_recv.at[z], 3 - z, c
+        )
+
     @when(z < 3)
     def _():
         ag_own(1).start()
@@ -219,6 +226,10 @@
         @when(z > 0)
         def _():
             ag(above, 0).start()
+
+    @when(is_end)
+    def _():
+        ag_direct().start()
 
     load_w[1].wait()
     project(z, 1)
@@ -229,14 +240,6 @@
     pair_sum(first, 0)
     ag(two_away, 0).wait_recv()
 
-    @when(z == 1)
-    def _():
-        ag(two_away, 0).start()
-
-    @when(z == 2)
-    def _():
-        ag(two_away, 1).start()
-
     project(second, 0)
     pair_sum(first, 1)
     project(second, 1)
@@ -294,7 +297,10 @@
     def norm_copy(b, at, to_c):
         return remote(norm_ref.at[b], norm_ref.at[b], n_send.at[at], n_recv.at[b], z, to_c)
 
-    norm_copy(c, 0, across).start()
+    @when(core == 0)
+    def _():
+        norm_copy(c, 0, across).start()
+
     norm_copy(c, 1, mate).start()
     load_rot.wait()
 
@@ -310,6 +316,12 @@
                 norm_copy(b, 2, mate).start()
 
         tiles(norm_ref, b, rot, rotp, q)
+        if b == block_order[0] and q == 0:
+
+            @when(core == 1)
+            def _():
+                norm_copy(c, 0, across).start()
+
 
     def piece(h, q):
         return pl.ds(pl.multiple_of(h * half + q * quarter, quarter), quarter)
@@ -475,11 +487,11 @@
 
     for s in range(4):
 
-        @when((s <= z) & (z < 3))
+        @when((s <= z) & (s >= z - 1) & (z < 3))
         def _():
             ag(s, 1).wait_send()
 
-        @when((s >= z) & (z > 0))
+        @when((s >= z) & (s <= z + 1) & (z > 0))
         def _():
             ag(s, 0).wait_send()
 
@@ -507,6 +519,10 @@
                 @when(z != s)
                 def _():
                     kurt_copy(u).wait_send()
+
+    @when(is_end)
+    def _():
+        ag_direct().wait_send()
 
     for q in (0, 1):
         x_copy(across, q).wait_send()
@@ -515,6 +531,27 @@
     norm_copy(c, 0, across).wait_send()
     norm_copy(c, 1, mate).wait_send()
     norm_copy(across, 2, mate).wait_send()
+
+
+def outer(root, norm_ref, grad_ref, kurt_ref, out_ref, kurt_row):
+    @pl.when(pl.program_id(0) == 0)
+    def _():
+        shape = kurt_ref.shape
+        on_diagonal = lax.broadcasted_iota(jnp.int32, shape, 0) == lax.broadcasted_iota(
+            jnp.int32, shape, 1
+        )
+        row = jnp.sum(jnp.where(on_diagonal, kurt_ref[...], 0.0), axis=0, keepdims=True)
+        kurt_row[...] = row[:, : kurt_row.shape[1]]
+
+    for i in range(out_ref.shape[1] // outer_cols):
+        cols = pl.ds(i * outer_cols, outer_cols)
+        out_ref[:, cols] = (
+            lax.dot_general(
+                norm_ref[...], grad_ref[:, cols], (((0,), (0,)), ((), ())),
+                preferred_element_type=jnp.float32,
+            )
+            / root
+        )
 
 
 def fused_shards(attn_out, residual, w_out, norm_gain, rotation):
@@ -548,17 +585,34 @@
             dma((6,)), dma((2, 4)), dma((4,)), dma((2, 2)), dma((2, 2)), dma((2,)), dma((2,)),
             dma((4,)), dma((4,)), dma((3,)), dma((4,)), dma((4, 2, 2)), dma((4, 2, 2)),
             dma((4, 2, 4)), dma((4, 2, 4)), dma((4, 2, 2)), dma((4, 2, 2)), dma((4, 2)), dma((2, 2)),
+            dma((1,)),
         ],
         compiler_params=pltpu.CompilerParams(
             collective_id=0, has_side_effects=True, vmem_limit_bytes=60 * 1024 * 1024
         ),
     )(attn_out, residual, norm_gain.reshape(1, width), w_out, rotation)
-    normed = normed.reshape(4 * block, width)
-    grads = grads.reshape(4 * block, width)
-    grad_rot = lax.dot_general(
-        normed, grads, (((0,), (0,)), ((), ())), preferred_element_type=jnp.float32
-    )
-    return (kurt[:, :, :, 0].reshape(block), grad_rot / math.sqrt(4 * block))
+    tokens = 4 * block
+    grad_rot, kurt_row = pl.pallas_call(
+        functools.partial(outer, math.sqrt(tokens)),
+        grid=(width // outer_rows,),
+        out_shape=(
+            jax.ShapeDtypeStruct((width, width), jnp.float32),
+            jax.ShapeDtypeStruct((1, block), jnp.float32),
+        ),
+        in_specs=[
+            pl.BlockSpec((tokens, outer_rows), lambda i: (0, i)),
+            pl.BlockSpec((tokens, width), lambda i: (0, 0)),
+            pl.BlockSpec((block, 128), lambda i: (0, 0)),
+        ],
+        out_specs=(
+            pl.BlockSpec((outer_rows, width), lambda i: (i, 0)),
+            pl.BlockSpec((1, block), lambda i: (0, 0)),
+        ),
+        cost_estimate=pl.CostEstimate(
+            flops=2 * tokens * width * width, bytes_accessed=4 * width * width, transcendentals=0
+        ),
+    )(normed.reshape(tokens, width), grads.reshape(tokens, width), kurt.reshape(block, 128))
+    return (kurt_row.reshape(block), grad_rot)
 
 
 def solution(mesh):

time: 115 us -> 119 us (1.035)
  Pallas kernels: 103 us -> 118 us
  matrix products: 10.1 us -> 0 us
  local copies, waits for them, and re-layouts: 1.45 us -> 0 us
    dot_general x1 -> x0, matrix products: 10.1 us -> none  [fused_shards(): lax.dot_general(normed, grads, (((0,), (0,)), ((), ())), preferred_elemen...]
    pallas_call x0 -> x1, Pallas kernels: none -> 9.57 us  [fused_shards(): pl.pallas_call(functools.partial(outer, math.sqrt(tokens)), grid=(width /...]
    pallas_call x1, Pallas kernels: 103 us -> 108 us  [fused_shards(): pl.pallas_call(functools.partial(kernel, full_width), out_shape=(jax.Shap...]
where the time goes in v3:
time: 119 us; the launch traced here: 118 us
  Pallas kernels  118 us (99%)
    pallas_call x1, Pallas kernels, fused_shards(): pl.pallas_call(functools.partial(kernel, full_width), out_shape=(jax.Shap...  108 us
    pallas_call x1, Pallas kernels, fused_shards(): pl.pallas_call(functools.partial(outer, math.sqrt(tokens)), grid=(width /...  9.57 us

profile of v3, /device:TPU:0, one launch (start us, length us, event | category | flops | bytes accessed | tf_op | source)
XLA Modules:
  0.0 118.3 jit_solution(530810237750644404)
XLA Ops:
  0.6 108.1 %shard_map.68 = (f32[2,2,16,128]{3,2,1,0:T(8,128)}, bf16[4,64,2048]{2,1,0:T(8,128)(2,1)}, bf16[4,64,2048]{2,1,0:T(8,128)(2,1)}) custom-call(bf16[64,2048]{1,0:T(8,128)(2,1)} %attn_hbm.1, bf16[64,2048]{1,0:T(8,128)(2,1)} %res_hbm.1, f32[1,2048]{1,0:T(1,128)} %bitcast.5, bf16[2048,2048]{1,0:T(8,128)(2,1)} %w_hbm.1, bf16[2048,2048]{1,0:T(8,128)(2,1)} %rot_hbm.1), custom_call_target="tpu_custom_call" | custom-call | tf_op jit(solution)/shard_map/pallas_call | solution.py:563
  108.7 9.6 %shard_map.69 = (f32[2048,2048]{1,0:T(8,128)}, f32[1,64]{1,0:T(1,128)}) custom-call(bf16[256,2048]{1,0:T(8,128)(2,1)} %bitcast.6, bf16[256,2048]{1,0:T(8,128)(2,1)} %bitcast.7, f32[64,128]{1,0:T(8,128)} %bitcast.8), custom_call_target="tpu_custom_call" | custom-call | flops 2147483648 | bytes 16777216 | tf_op jit(solution)/shard_map/pallas_call | solution.py:595
